TPU v7x, 32 devices: a whole 2x2x4 slice. The times are simulated.
32 devices in a mesh: kx: 4 (over y, core), ky: 8 (over z, x).
Axes of the slice: x: 2, y: 2, z: 4, core: 2. Of those that a mesh axis runs over, the one named last changes fastest.
Arguments:
- packed_state_matrix: float32 [16, 128, 1024], P(None, 'kx', 'ky'), may hold values from -1 to 1, as said below
- energies: float32 [4, 128, 1024], P(None, 'kx', 'ky'), may hold values from -2.4 to 2.4
- dipole_x: float32 [12, 128, 1024], P(None, 'kx', 'ky'), may hold values from -2.5 to 2.5
- dipole_y: float32 [12, 128, 1024], P(None, 'kx', 'ky'), may hold values from -2.5 to 2.5
- interaction: float32 [128, 1024], P('ky'), may hold values from 0.3 to 5, as said below
- driving_field: float32 [2], replicated, may hold values from 0.3 to 1
Outputs:
- section_slope: float32 [16, 128, 1024], P(None, 'kx', 'ky')
- field_next: float32 [2], replicated
Inputs may be any that keep to these rules, and one draw needn't show every extreme that they name: `packed_state_matrix`: components 0 to 3 lie in 0 to 1. interaction at (p, q) equals interaction at ((-p) mod 128, q) and at (p, (-q) mod 1024).
All inputs are finite; a program needn't handle non-finite values.
Results may differ from a plain program's by a relative error of at most 0.000054.
Values sent between devices are 32-bit elements; how exact they have to be, the bound alone decides.
A program may use at most 64 MiB of HBM per device.

v0:
```python
from functools import partial
import math

import jax
import jax.numpy as jnp
from jax import lax
from jax.sharding import PartitionSpec as P

BAND_PAIRS = ((0, 1), (0, 2), (0, 3), (1, 2), (1, 3), (2, 3))
DEPHASING = 0.5
SHIELDING_LEVEL = 2.0
COUPLING = 40.0


def with_halo(array, sides, width):
    for axis, dim in sides:
        devices, length = (lax.axis_size(axis), array.shape[dim])
        up = [(i, (i + 1) % devices) for i in range(devices)]
        down = [(j, i) for i, j in up]
        last = lax.slice_in_dim(array, length - width, length, axis=dim)
        initial = lax.slice_in_dim(array, 0, width, axis=dim)
        before = lax.ppermute(last, axis, up)
        after = lax.ppermute(initial, axis, down)
        array = jnp.concatenate([before, array, after], axis=dim)
    return array


def unpack(packed):
    real_entries = []
    imaginary_entries = []
    for band_one in range(4):
        real_entries.append([None, None, None, None])
        imaginary_entries.append([None, None, None, None])
    for band_one in range(4):
        real_entries[band_one][band_one] = packed[band_one]
    for number, band_pair in enumerate(BAND_PAIRS):
        upper_band, lower_band = band_pair
        real_entries[upper_band][lower_band] = packed[4 + number]
        real_entries[lower_band][upper_band] = packed[4 + number]
        imaginary_entries[upper_band][lower_band] = packed[10 + number]
        imaginary_entries[lower_band][upper_band] = -packed[10 + number]
    return (real_entries, imaginary_entries)


def product_sum(terms):
    summed = None
    for factor, left_value, right_value in terms:
        if left_value is None or right_value is None:
            continue
        product = factor * left_value * right_value
        summed = product if summed is None else summed + product
    return summed


def commutator(coupled, packed_state_matrix):
    coupled_real, coupled_imaginary = unpack(coupled)
    state_real, state_imaginary = unpack(packed_state_matrix)

    def element(row_band, column_band):
        real_terms = []
        imaginary_terms = []
        for middle in range(4):
            real_terms.append(
                (1.0, coupled_real[row_band][middle], state_real[middle][column_band])
            )
            real_terms.append(
                (-1.0, coupled_imaginary[row_band][middle], state_imaginary[middle][column_band])
            )
            real_terms.append(
                (-1.0, state_real[row_band][middle], coupled_real[middle][column_band])
            )
            real_terms.append(
                (1.0, state_imaginary[row_band][middle], coupled_imaginary[middle][column_band])
            )
            imaginary_terms.append(
                (1.0, coupled_real[row_band][middle], state_imaginary[middle][column_band])
            )
            imaginary_terms.append(
                (1.0, coupled_imaginary[row_band][middle], state_real[middle][column_band])
            )
            imaginary_terms.append(
                (-1.0, state_real[row_band][middle], coupled_imaginary[middle][column_band])
            )
            imaginary_terms.append(
                (-1.0, state_imaginary[row_band][middle], coupled_real[middle][column_band])
            )
        return (product_sum(real_terms), product_sum(imaginary_terms))

    diagonal = []
    upper_real = []
    upper_imaginary = []
    for band_one in range(4):
        diagonal.append(element(band_one, band_one)[1])
    for upper_band, lower_band in BAND_PAIRS:
        real_value, imaginary_value = element(upper_band, lower_band)
        upper_real.append(imaginary_value)
        upper_imaginary.append(-real_value)
    return jnp.stack(diagonal + upper_real + upper_imaginary)


def slope_terms(
    packed_state_matrix,
    energies,
    self_energy,
    gradient_x,
    gradient_y,
    dipole_x,
    dipole_y,
    driving_field,
):
    field_x = driving_field[0]
    field_y = driving_field[1]
    coupled = jnp.concatenate(
        [energies + self_energy[0:4], self_energy[4:16] + field_x * dipole_x + field_y * dipole_y]
    )
    rotation = commutator(coupled, packed_state_matrix)
    drift = rotation + field_x * gradient_x + field_y * gradient_y
    return jnp.concatenate([drift[0:4], drift[4:16] - DEPHASING * packed_state_matrix[4:16]])


def angle_table(row_count, column_count, period, direction):
    row_index = lax.broadcasted_iota(jnp.int32, (row_count, column_count), 0)
    column_index = lax.broadcasted_iota(jnp.int32, (row_count, column_count), 1)
    phase_angle = (row_index * column_index % period).astype(jnp.float32) * (
        direction * 2.0 * math.pi / period
    )
    return (jnp.cos(phase_angle), jnp.sin(phase_angle))


def complex_contract(einsum_form, data_real, data_imaginary, table_real, table_imaginary):
    contract = partial(
        jnp.einsum, precision=lax.Precision.HIGHEST, preferred_element_type=jnp.float32
    )
    if data_imaginary is None:
        return (
            contract(einsum_form, data_real, table_real),
            contract(einsum_form, data_real, table_imaginary),
        )
    real_out = contract(einsum_form, data_real, table_real) - contract(
        einsum_form, data_imaginary, table_imaginary
    )
    imaginary_out = contract(einsum_form, data_real, table_imaginary) + contract(
        einsum_form, data_imaginary, table_real
    )
    return (real_out, imaginary_out)


def transform(data_real, data_imaginary, direction, along_last):
    length = data_real.shape[-1] if along_last else data_real.shape[-2]
    outer_size = 16
    inner_size = length // outer_size
    outer_cosine, outer_sine = angle_table(outer_size, outer_size, outer_size, direction)
    twist_cosine, twist_sine = angle_table(outer_size, inner_size, length, direction)
    inner_cosine, inner_sine = angle_table(inner_size, inner_size, inner_size, direction)
    if along_last:
        split_shape = data_real.shape[:-1] + (outer_size, inner_size)
        first_form = "...aq,ab->...bq"
        second_form = "...bq,qc->...cb"
    else:
        split_shape = data_real.shape[:-2] + (outer_size, inner_size, data_real.shape[-1])
        first_form = "...aqt,ab->...bqt"
        second_form = "...bqt,qc->...cbt"
        twist_cosine = twist_cosine[:, :, None]
        twist_sine = twist_sine[:, :, None]
    part_real = data_real.reshape(split_shape)
    part_imaginary = None if data_imaginary is None else data_imaginary.reshape(split_shape)
    section_real, section_imaginary = complex_contract(
        first_form, part_real, part_imaginary, outer_cosine, outer_sine
    )
    turned_real = section_real * twist_cosine - section_imaginary * twist_sine
    turned_imaginary = section_real * twist_sine + section_imaginary * twist_cosine
    final_real, final_imaginary = complex_contract(
        second_form, turned_real, turned_imaginary, inner_cosine, inner_sine
    )
    return (final_real.reshape(data_real.shape), final_imaginary.reshape(data_real.shape))


def convolve(source, interaction, primitive_tile_total):
    along_kx = lax.all_to_all(source, "kx", split_axis=0, concat_axis=1, tiled=True)
    broad_nonimaginary, wide_imaginary = transform(along_kx, None, -1.0, False)
    joined = jnp.stack([broad_nonimaginary, wide_imaginary])
    along_ky = lax.all_to_all(joined, "ky", split_axis=2, concat_axis=3, tiled=True)
    line_real, line_imaginary = transform(along_ky[0], along_ky[1], -1.0, True)
    line_real, line_imaginary = transform(
        line_real * interaction, line_imaginary * interaction, 1.0, True
    )
    returned = lax.all_to_all(
        jnp.stack([line_real, line_imaginary]), "ky", split_axis=3, concat_axis=2, tiled=True
    )
    final_real, final_imaginary = transform(returned[0], returned[1], 1.0, False)
    normalizer = 1.0 / primitive_tile_total
    return lax.all_to_all(final_real * normalizer, "kx", split_axis=1, concat_axis=0, tiled=True)


def collect_moments(local_sums, primitive_tile_total):
    return lax.psum(local_sums, ("kx", "ky")) / primitive_tile_total


def body(packed_state_matrix, energies, dipole_x, dipole_y, interaction, driving_field):
    rows_local = packed_state_matrix.shape[1]
    columns_local = packed_state_matrix.shape[2]
    primitive_tile_total = rows_local * columns_local * lax.axis_size("kx") * lax.axis_size("ky")
    stacked = jnp.concatenate([packed_state_matrix, energies])
    padded = with_halo(stacked, (("kx", 1), ("ky", 2)), 2)
    column_core = padded[:, :, 2:-2]
    row_core = padded[:, 2:-2, :]
    gradient_x = (
        8.0 * (column_core[:, 3:-1] - column_core[:, 1:-3])
        - (column_core[:, 4:] - column_core[:, :-4])
    ) / 12.0
    gradient_y = (
        8.0 * (row_core[:, :, 3:-1] - row_core[:, :, 1:-3])
        - (row_core[:, :, 4:] - row_core[:, :, :-4])
    ) / 12.0
    populations = packed_state_matrix[0:4]
    local_sums = jnp.stack(
        [
            jnp.sum(packed_state_matrix[2] + packed_state_matrix[3]),
            jnp.sum(gradient_x[16:20] * populations),
            jnp.sum(gradient_y[16:20] * populations),
        ]
    )
    totals = collect_moments(local_sums, primitive_tile_total)
    shielding_multiplier = 1.0 / (1.0 + SHIELDING_LEVEL * totals[0])
    self_energy = -convolve(
        packed_state_matrix * shielding_multiplier, interaction, primitive_tile_total
    )
    section_slope = slope_terms(
        packed_state_matrix,
        energies,
        self_energy,
        gradient_x[0:16],
        gradient_y[0:16],
        dipole_x,
        dipole_y,
        driving_field,
    )
    field_next = driving_field - COUPLING * totals[1:3]
    return (section_slope, field_next)


def solution(mesh):
    in_specs = (
        P(None, "kx", "ky"),
        P(None, "kx", "ky"),
        P(None, "kx", "ky"),
        P(None, "kx", "ky"),
        P("ky", None),
        P(),
    )
    out_specs = (P(None, "kx", "ky"), P())
    return jax.shard_map(body, mesh=mesh, in_specs=in_specs, out_specs=out_specs, check_vma=False)
```

profile of v0, /device:TPU:0, one launch (start us, length us, event | category | flops | bytes accessed | tf_op | source)
XLA Modules:
  0.0 191.4 jit_solution(13636346387585526352)
XLA Ops:
  0.6 1.0 constant_dynamic-update-slice_fusion.1
  1.6 0.8 constant_dynamic-update-slice_fusion
  2.5 2.5 %collective-permute-start = (f32[20,2,128]{2,1,0:T(2,128)S(1)}, f32[20,2,128]{2,1,0:T(2,128)S(1)}, u32[]{:S(2)}, u32[]{:S(2)}) collective-permute-start(f32[20,2,128]{2,1,0:T(2,128)S(1)} %get-tuple-element.15), channel_id=1, source_target_pairs={{8,0},{16,8},{24,16},{0,24},{9,1},{17,9},{25,17},{1,25},{10,2},{18... | collective-permute-start | bytes 61448 | tf_op jit(solution)/shard_map/ppermute | solution.py:23
  4.9 1.4 add_reduce_fusion
  6.4 1.7 collective-permute-done.1
  8.4 4.6 %collective-permute-start.2 = (f32[20,36,2]{2,1,0:T(8,128)S(1)}, f32[20,36,2]{2,1,0:T(8,128)S(1)}, u32[]{:S(2)}, u32[]{:S(2)}) collective-permute-start(f32[20,36,2]{2,1,0:T(8,128)S(1)} %get-tuple-element.12), channel_id=1, source_target_pairs={{1,0},{2,1},{3,2},{4,3},{5,4},{6,5},{7,6},{0,7},{9,8},{10,9},{11,1... | collective-permute-start | bytes 17288 | tf_op jit(solution)/shard_map/ppermute | solution.py:23
  13.2 14.4 %collective-permute-done.2 = f32[20,36,2]{2,1,0:T(8,128)S(1)} collective-permute-done((f32[20,36,2]{2,1,0:T(8,128)S(1)}, f32[20,36,2]{2,1,0:T(8,128)S(1)}, u32[]{:S(2)}, u32[]{:S(2)}) %collective-permute-start.2) | collective-permute-done | bytes 5792 | tf_op jit(solution)/shard_map/ppermute | solution.py:23
  27.5 0.7 fusion.34
  28.3 0.6 fusion.65
  29.1 2.0 %pad_maximum_fusion.12 = f32[3]{0:T(128)S(1)} fusion(f32[1]{0:T(128)} %bitcast.16, f32[1]{0:T(128)} %bitcast.15, f32[1]{0:T(128)} %bitcast.14), kind=kLoop, calls=%fused_computation.256 | loop fusion | flops 6 | bytes 24 | tf_op jit(solution)/shard_map/stack | solution.py:216
  31.1 41.2 %psum.7 = f32[3]{0:T(128)S(1)} all-reduce(f32[3]{0:T(128)S(1)} %pad_maximum_fusion.12), channel_id=1, replica_groups=mesh['kx'=4,'ky'=8] {'kx','ky'}, use_global_device_ids=true, to_apply=%region_3.0 | all-reduce | flops 3 | bytes 24 | tf_op jit(solution)/shard_map/psum | solution.py:196
  72.9 0.7 broadcast_multiply_fusion
  73.6 3.5 %all-to-all-start = ((f32[16,32,128]{2,1,0:T(8,128)}), f32[16,32,128]{2,1,0:T(8,128)S(1)}, u32[]{:S(2)}, u32[]{:S(2)}) async-start(f32[16,32,128]{2,1,0:T(8,128)} %broadcast_multiply_fusion), calls=%async_computation | async-start | bytes 524288 | tf_op jit(solution)/shard_map/all_to_all | solution.py:179
  77.2 6.0 %all-to-all-done = f32[16,32,128]{2,1,0:T(8,128)S(1)} async-done(((f32[16,32,128]{2,1,0:T(8,128)}), f32[16,32,128]{2,1,0:T(8,128)S(1)}, u32[]{:S(2)}, u32[]{:S(2)}) %all-to-all-start) | async-done | bytes 262176 | tf_op jit(solution)/shard_map/all_to_all | solution.py:179
  86.0 1.2 copy.98
  87.1 5.2 %all-to-all-start.1 = ((f32[2,4,128,128]{3,1,0,2:T(4,128)}), f32[2,4,128,128]{3,1,0,2:T(4,128)S(1)}, u32[]{:S(2)}, u32[]{:S(2)}) async-start(f32[2,4,128,128]{3,1,0,2:T(4,128)} %copy.98), calls=%async_computation.1 | async-start | bytes 1048576 | tf_op jit(solution)/shard_map/all_to_all | solution.py:182
  92.5 14.1 %all-to-all-done.1 = f32[2,4,128,128]{3,1,0,2:T(4,128)S(1)} async-done(((f32[2,4,128,128]{3,1,0,2:T(4,128)}), f32[2,4,128,128]{3,1,0,2:T(4,128)S(1)}, u32[]{:S(2)}, u32[]{:S(2)}) %all-to-all-start.1) | async-done | bytes 524320 | tf_op jit(solution)/shard_map/all_to_all | solution.py:182
  109.7 1.5 fusion.16
  111.2 0.7 fusion.18
  112.0 1.5 fusion.3
  113.5 1.7 copy.102
  115.1 1.3 reshape.119
  116.4 2.5 %fusion.24 = f32[16,4,16,64]{3,0,2,1:T(8,128)} fusion(f32[4,16,16,64]{3,2,1,0:T(8,128)} %reshape.119, f32[16,16,64]{2,1,0:T(8,128)S(1)} %mul.1558), kind=kOutput, calls=%fused_computation.43 | convolution fusion | flops 12652032 | bytes 589824 | tf_op jit(solution)/shard_map/...aq,ab->...bq/dot_general | solution.py:139
  119.0 1.6 fusion.22
  120.6 0.7 fusion.2
  122.5 1.7 convolution_subtract_fusion.1
  124.1 0.6 convolution_add_fusion.1
  124.8 0.7 fusion.12
  125.5 1.5 fusion.10
  127.0 1.8 fusion.1
  128.8 1.7 copy.104
  130.4 2.3 %stack_reshape.14 = f32[1,4,16,1024]{3,2,1,0:T(8,128)} reshape(f32[4,16,64,16]{3,2,1,0:T(8,128)S(1)} %copy.104) | data formatting | bytes 524288 | tf_op jit(solution)/shard_map/stack;reshape | solution.py:188
  132.7 1.7 fusion
  135.1 1.6 stack_reshape.15
  136.7 3.1 %copy.106 = f32[2,4,16,1024]{2,1,0,3:T(4,128)} copy(f32[2,4,16,1024]{3,2,1,0:T(8,128)S(1)} %pad_maximum_fusion.1) | data formatting | bytes 1048576 | tf_op jit(solution)/shard_map/stack | solution.py:188
  139.7 5.4 %reshape.133 = f32[8,1,16384]{2,1,0:T(1,128)} reshape(f32[1024,2,4,16]{3,2,1,0:T(4,128)} %bitcast.188) | data formatting | bytes 1048576
  145.2 3.8 %all-to-all-start.2 = ((f32[8,1,16384]{2,1,0:T(1,128)}), f32[8,1,16384]{2,1,0:T(1,128)S(1)}, u32[]{:S(2)}, u32[]{:S(2)}) async-start(f32[8,1,16384]{2,1,0:T(1,128)} %reshape.133), calls=%async_computation.2 | async-start | bytes 1048576 | tf_op jit(solution)/shard_map/all_to_all | solution.py:187
  148.9 0.7 fusion.297
  149.6 13.7 %all-to-all-done.2 = f32[8,1,16384]{2,1,0:T(1,128)S(1)} async-done(((f32[8,1,16384]{2,1,0:T(1,128)}), f32[8,1,16384]{2,1,0:T(1,128)S(1)}, u32[]{:S(2)}, u32[]{:S(2)}) %all-to-all-start.2) | async-done | bytes 524320 | tf_op jit(solution)/shard_map/all_to_all | solution.py:187
  163.8 1.9 reduce.1
  165.7 4.9 %reshape.134 = f32[1024,2,4,16]{3,2,1,0:T(4,128)} reshape(f32[8,16384]{1,0:T(8,128)S(1)} %reduce.1) | data formatting | bytes 1048576
  170.6 2.8 %copy.132 = f32[2,4,16,8,128]{4,3,2,1,0:T(8,128)S(1)} copy(f32[2,4,16,8,128]{2,1,0,4,3:T(4,128)} %bitcast.189) | data formatting | bytes 1048576 | tf_op jit(solution)/shard_map/all_to_all | solution.py:187
  176.2 0.9 copy.117
  177.1 3.4 %all-to-all-start.3 = ((f32[4,128,128]{2,0,1:T(4,128)}), f32[4,128,128]{2,0,1:T(4,128)S(1)}, u32[]{:S(2)}, u32[]{:S(2)}) async-start(f32[4,128,128]{2,0,1:T(4,128)} %copy.117), calls=%async_computation.3 | async-start | bytes 524288 | tf_op jit(solution)/shard_map/all_to_all | solution.py:192
  181.1 5.4 %all-to-all-done.3 = f32[4,128,128]{2,0,1:T(4,128)S(1)} async-done(((f32[4,128,128]{2,0,1:T(4,128)}), f32[4,128,128]{2,0,1:T(4,128)S(1)}, u32[]{:S(2)}, u32[]{:S(2)}) %all-to-all-start.3) | async-done | bytes 262176 | tf_op jit(solution)/shard_map/all_to_all | solution.py:192
  186.7 1.4 fusion.62
  189.3 1.4 fusion.37
  190.7 0.7 pad_maximum_fusion.11
  (108 shorter events, 14.1 us)
Async XLA Ops:
  2.5 3.9 %collective-permute-start = (f32[20,2,128]{2,1,0:T(2,128)S(1)}, f32[20,2,128]{2,1,0:T(2,128)S(1)}, u32[]{:S(2)}, u32[]{:S(2)}) collective-permute-start(f32[20,2,128]{2,1,0:T(2,128)S(1)} %get-tuple-element.15), channel_id=1, source_target_pairs={{8,0},{16,8},{24,16},{0,24},{9,1},{17,9},{25,17},{1,25},{10,2},{18... | collective-permute-start | bytes 61448 | tf_op jit(solution)/shard_map/ppermute | solution.py:23
  4.9 3.2 %collective-permute-start.1 = (f32[20,2,128]{2,1,0:T(2,128)S(1)}, f32[20,2,128]{2,1,0:T(2,128)S(1)}, u32[]{:S(2)}, u32[]{:S(2)}) collective-permute-start(f32[20,2,128]{2,1,0:T(2,128)S(1)} %get-tuple-element.14), channel_id=1, source_target_pairs={{0,8},{8,16},{16,24},{24,0},{1,9},{9,17},{17,25},{25,1},{2,10},{10... | collective-permute-start | bytes 61448 | tf_op jit(solution)/shard_map/ppermute | solution.py:22
  8.2 20.1 %copy-start = (f32[16,32,128]{2,1,0:T(8,128)S(1)}, f32[16,32,128]{2,1,0:T(8,128)}, u32[]{:S(2)}) copy-start(f32[16,32,128]{2,1,0:T(8,128)} %param.6) | copy-start | bytes 786436
  8.4 19.1 %collective-permute-start.2 = (f32[20,36,2]{2,1,0:T(8,128)S(1)}, f32[20,36,2]{2,1,0:T(8,128)S(1)}, u32[]{:S(2)}, u32[]{:S(2)}) collective-permute-start(f32[20,36,2]{2,1,0:T(8,128)S(1)} %get-tuple-element.12), channel_id=1, source_target_pairs={{1,0},{2,1},{3,2},{4,3},{5,4},{6,5},{7,6},{0,7},{9,8},{10,9},{11,1... | collective-permute-start | bytes 17288 | tf_op jit(solution)/shard_map/ppermute | solution.py:23
  13.0 14.6 %collective-permute-start.3 = (f32[20,36,2]{2,1,0:T(8,128)S(1)}, f32[20,36,2]{2,1,0:T(8,128)S(1)}, u32[]{:S(2)}, u32[]{:S(2)}) collective-permute-start(f32[20,36,2]{2,1,0:T(8,128)S(1)} %get-tuple-element.13), channel_id=1, source_target_pairs={{0,1},{1,2},{2,3},{3,4},{4,5},{5,6},{6,7},{7,0},{8,9},{9,10},{10,1... | collective-permute-start | bytes 17288 | tf_op jit(solution)/shard_map/ppermute | solution.py:22
  13.2 15.1 %copy-start.2 = (f32[20,32,128]{2,1,0:T(8,128)}, f32[20,32,128]{2,1,0:T(8,128)S(1)}, u32[]{:S(2)}) copy-start(f32[20,32,128]{2,1,0:T(8,128)S(1)} %fusion.30) | copy-start | bytes 983044
  28.3 0.7 copy-start.4
  72.3 0.6 copy-start.16
  73.6 9.6 %all-to-all-start = ((f32[16,32,128]{2,1,0:T(8,128)}), f32[16,32,128]{2,1,0:T(8,128)S(1)}, u32[]{:S(2)}, u32[]{:S(2)}) async-start(f32[16,32,128]{2,1,0:T(8,128)} %broadcast_multiply_fusion), calls=%async_computation | async-start | bytes 524288 | tf_op jit(solution)/shard_map/all_to_all | solution.py:179
  85.4 6.9 %copy-start.14 = (f32[16,1024]{1,0:T(8,128)S(1)}, f32[16,1024]{1,0:T(8,128)}, u32[]{:S(2)}) copy-start(f32[16,1024]{1,0:T(8,128)} %param.10) | copy-start | bytes 196612
  87.1 19.5 %all-to-all-start.1 = ((f32[2,4,128,128]{3,1,0,2:T(4,128)}), f32[2,4,128,128]{3,1,0,2:T(4,128)S(1)}, u32[]{:S(2)}, u32[]{:S(2)}) async-start(f32[2,4,128,128]{3,1,0,2:T(4,128)} %copy.98), calls=%async_computation.1 | async-start | bytes 1048576 | tf_op jit(solution)/shard_map/all_to_all | solution.py:182
  92.4 19.5 %copy-start.8 = (f32[16,64]{1,0:T(8,128)}, f32[16,64]{1,0:T(8,128)S(1)}, u32[]{:S(2)}) copy-start(f32[16,64]{1,0:T(8,128)S(1)} %get-tuple-element.20) | copy-start | bytes 12292
  92.5 19.5 %copy-start.10 = (f32[16,64]{1,0:T(8,128)}, f32[16,64]{1,0:T(8,128)S(1)}, u32[]{:S(2)}) copy-start(f32[16,64]{1,0:T(8,128)S(1)} %get-tuple-element.21) | copy-start | bytes 12292
  116.4 4.2 %copy-start.1 = (f32[64,4,16,16]{0,3,2,1:T(8,128)S(1)}, f32[64,4,16,16]{0,3,2,1:T(8,128)}, u32[]{:S(2)}) copy-start(f32[64,4,16,16]{0,3,2,1:T(8,128)} %fusion.16) | copy-start | bytes 786436
  116.4 4.2 %copy-start.9 = (f32[16,64]{1,0:T(8,128)S(1)}, f32[16,64]{1,0:T(8,128)}, u32[]{:S(2)}) copy-start(f32[16,64]{1,0:T(8,128)} %copy-done.8) | copy-start | bytes 12292
  116.4 4.2 %copy-start.11 = (f32[16,64]{1,0:T(8,128)S(1)}, f32[16,64]{1,0:T(8,128)}, u32[]{:S(2)}) copy-start(f32[16,64]{1,0:T(8,128)} %copy-done.10) | copy-start | bytes 12292
  134.4 2.2 %copy-start.6 = (f32[1,4,16,1024]{3,2,1,0:T(8,128)S(1)}, f32[1,4,16,1024]{3,2,1,0:T(8,128)}, u32[]{:S(2)}) copy-start(f32[1,4,16,1024]{3,2,1,0:T(8,128)} %stack_reshape.14) | copy-start | bytes 786436
  139.7 9.2 %copy-start.15 = (f32[2]{0:T(128)S(1)}, f32[2]{0:T(128)}, u32[]{:S(2)}) copy-start(f32[2]{0:T(128)} %param.11) | copy-start | bytes 28
  145.2 18.2 %all-to-all-start.2 = ((f32[8,1,16384]{2,1,0:T(1,128)}), f32[8,1,16384]{2,1,0:T(1,128)S(1)}, u32[]{:S(2)}, u32[]{:S(2)}) async-start(f32[8,1,16384]{2,1,0:T(1,128)} %reshape.133), calls=%async_computation.2 | async-start | bytes 1048576 | tf_op jit(solution)/shard_map/all_to_all | solution.py:187
  174.8 5.7 %copy-start.17 = (f32[3]{0:T(128)S(1)}, f32[3]{0:T(128)}, u32[]{:S(2)}) copy-start(f32[3]{0:T(128)} %copy-done.16) | copy-start | bytes 40
  175.3 11.3 %copy-start.7 = (f32[4,32,128]{2,1,0:T(8,128)S(1)}, f32[4,32,128]{2,1,0:T(8,128)}, u32[]{:S(2)}) copy-start(f32[4,32,128]{2,1,0:T(8,128)} %param.7) | copy-start | bytes 196612
  175.3 11.3 %copy-start.12 = (f32[12,32,128]{2,1,0:T(8,128)S(1)}, f32[12,32,128]{2,1,0:T(8,128)}, u32[]{:S(2)}) copy-start(f32[12,32,128]{2,1,0:T(8,128)} %param.9) | copy-start | bytes 589828
  175.3 11.3 %copy-start.13 = (f32[12,32,128]{2,1,0:T(8,128)S(1)}, f32[12,32,128]{2,1,0:T(8,128)}, u32[]{:S(2)}) copy-start(f32[12,32,128]{2,1,0:T(8,128)} %param.8) | copy-start | bytes 589828
  177.1 9.4 %all-to-all-start.3 = ((f32[4,128,128]{2,0,1:T(4,128)}), f32[4,128,128]{2,0,1:T(4,128)S(1)}, u32[]{:S(2)}, u32[]{:S(2)}) async-start(f32[4,128,128]{2,0,1:T(4,128)} %copy.117), calls=%async_computation.3 | async-start | bytes 524288 | tf_op jit(solution)/shard_map/all_to_all | solution.py:192
  188.2 1.0 copy-start.3
  188.2 1.1 copy-start.5
where the time goes:
time: 192 us; the launch traced here: 191 us
  waiting for transfers between devices  55.3 us (29%)
  blocking collectives  41.2 us (21%)
  local copies, waits for them, and re-layouts  34 us (18%)
  matrix products  24.1 us (13%)
  starting transfers between devices  22.9 us (12%)
  other arithmetic  12.6 us (7%)
    psum x1, blocking collectives, collect_moments(): return lax.psum(local_sums, ('kx', 'ky')) / primitive_tile_total  41.2 us
    ppermute x2, waiting for transfers between devices, with_halo(): after = lax.ppermute(initial, axis, down)  14.4 us
    all_to_all x1, waiting for transfers between devices, convolve(): lax.all_to_all(joined, 'ky', split_axis=2, concat_axis=3, tiled=True)  14.1 us
    all_to_all x1, waiting for transfers between devices, convolve(): lax.all_to_all(jnp.stack([line_real, line_imaginary]), 'ky', split_axis=3...  13.7 us
    unnamed x39, local copies, waits for them, and re-layouts  12.7 us
    ppermute x2, starting transfers between devices, with_halo(): after = lax.ppermute(initial, axis, down)  7.04 us
    another operation x3, local copies, waits for them, and re-layouts, convolve(): jnp.stack([line_real, line_imaginary])  6.88 us
    dot_general x7, matrix products, complex_contract(): contract(einsum_form, data_imaginary, table_imaginary)  6.84 us
  transfers between devices with their start and end apart: 8, of which 7 were waited for; matrix products, arithmetic and copies ran while one was open for 2% of the time, Pallas kernels for 0%

commit v1 on v0

--- a/solution.py
+++ b/solution.py
@@ -3,7 +3,11 @@
 
 import jax
 import jax.numpy as jnp
+import ml_dtypes
+import numpy as np
 from jax import lax
+from jax.experimental import pallas as pl
+from jax.experimental.pallas import tpu as pltpu
 from jax.sharding import PartitionSpec as P
 
 BAND_PAIRS = ((0, 1), (0, 2), (0, 3), (1, 2), (1, 3), (2, 3))
@@ -239,6 +243,591 @@
     return (section_slope, field_next)
 
 
+def split_table(values):
+    high = values.astype(ml_dtypes.bfloat16)
+    low = (values - high.astype(np.float64)).astype(ml_dtypes.bfloat16)
+    return high, low
+
+
+def kx_table(upper):
+    length = 128
+    x = np.arange(length)
+    rows = []
+    for half in range(2):
+        positions = np.arange(32 * half, 32 * half + 32)
+        if upper:
+            orders = 16 * (positions // 16) + 16 - positions % 16
+        else:
+            orders = positions
+        cosine = np.cos(2 * np.pi * (np.outer(orders, x) % length) / length)
+        sine = np.sin(2 * np.pi * (np.outer(orders, x) % length) / length)
+        cosine *= np.where((orders == 0) | (orders == 64), 1.0, np.sqrt(2.0))[:, None]
+        sine *= np.sqrt(2.0)
+        for at, order in enumerate(orders):
+            if not upper and order == 0:
+                sine[at] = np.where(x % 2 == 0, 1.0, -1.0)
+            if upper and order == 64:
+                sine[at] = 1.0
+        rows += [cosine, sine]
+    return np.concatenate(rows) / np.sqrt(length)
+
+
+def ky_tables():
+    length = 1024
+    k = np.arange(512)[:, None]
+
+    def waves(orders, reach):
+        angle = 2 * np.pi * (k[:reach] * orders[None, :] % length) / length
+        return np.cos(angle), np.sin(angle)
+
+    m = np.arange(128)
+    scale = np.sqrt(2.0 / length)
+    cosine, sine = waves(4 * m, 256)
+    cosine, sine = cosine * scale, sine * scale
+    cosine[:, 0] = np.sqrt(1.0 / length)
+    sine[:, 0] = np.where(np.arange(256) % 2 == 0, 1.0, -1.0) * np.sqrt(1.0 / length)
+    first = np.concatenate([cosine, sine], axis=1)
+    cosine, sine = waves(4 * m + 2, 256)
+    second = np.concatenate([cosine, sine], axis=1) * scale
+    cosine, sine = waves(4 * np.arange(256) + 1, 512)
+    third = np.concatenate([cosine, sine], axis=1) * scale
+    return first, second, third
+
+
+def pick_table():
+    m = np.arange(128)
+    wanted = np.concatenate([4 * m, 4 * m + 2, 4 * np.arange(256) + 1, np.full(128, 512)])
+    table = np.zeros((1024, 640))
+    table[wanted, np.arange(640)] = 1.0
+    return table
+
+
+MESH = pl.DeviceIdType.MESH
+COMPONENTS = 16
+ROWS, COLUMNS = 32, 128
+KX_DEVICES, KY_DEVICES = 4, 8
+
+
+def fits_section_kernel(mesh):
+    return (mesh.shape["kx"], mesh.shape["ky"]) == (KX_DEVICES, KY_DEVICES)
+
+
+def bf16_parts(values):
+    high = values.astype(jnp.bfloat16)
+    low = (values - high.astype(jnp.float32)).astype(jnp.bfloat16)
+    return high, low
+
+
+def matmul(left, right):
+    return jnp.dot(left, right, preferred_element_type=jnp.float32)
+
+
+def rows_by_table(values, table_high, table_low):
+    count = values.shape[0]
+    high, low = bf16_parts(values)
+    both = matmul(jnp.concatenate([high, low], axis=0), table_high)
+    return both[:count] + both[count:] + matmul(high, table_low)
+
+
+def table_by_columns(table, values):
+    high, low = bf16_parts(values)
+    return matmul(table, jnp.concatenate([high, low, high], axis=0))
+
+
+def section_kernel(
+    rho, energies, dipole_x, dipole_y, interaction, field,
+    kx_forward, kx_back, ky_short, ky_long, pick,
+    out, field_out,
+    lines, conv, halo_out, halo_in, columns_out, columns_in, extended,
+    weights_own, weights, weight_special, turned, turned_in, back, final,
+    sums_kx, sums_ky, static_part,
+    short_table, long_table, pick_table_vmem,
+    table_sem, send_sem, line_sem, halo_send, halo_recv, weight_send, weight_recv,
+    pair_send, pair_recv, return_send, return_recv, sum_send, sum_recv,
+):
+    i = lax.axis_index("kx")
+    j = lax.axis_index("ky")
+    chip_y = i // 2
+    half = i % 2
+    upper = j // 4
+    component = chip_y * 8 + j
+
+    tables = [
+        pltpu.make_async_copy(pick, pick_table_vmem, table_sem.at[0]),
+        pltpu.make_async_copy(ky_short, short_table, table_sem.at[1]),
+        pltpu.make_async_copy(ky_long, long_table, table_sem.at[2]),
+    ]
+    for table in tables:
+        table.start()
+
+    barrier = pltpu.get_barrier_semaphore()
+
+    def greet(device, carry):
+        @pl.when(device != i * KY_DEVICES + j)
+        def _():
+            pl.semaphore_signal(
+                barrier, inc=1, device_id=(device // KY_DEVICES, device % KY_DEVICES), device_id_type=MESH
+            )
+
+        return carry
+
+    lax.fori_loop(0, KX_DEVICES * KY_DEVICES, greet, 0)
+
+    def remote(source, target, send, receive, device):
+        return pltpu.make_async_remote_copy(
+            src_ref=source, dst_ref=target, send_sem=send, recv_sem=receive,
+            device_id=device, device_id_type=MESH,
+        )
+
+    def await_bytes(ref, semaphore):
+        pltpu.make_async_copy(ref, ref, semaphore).wait()
+
+    lane = lax.broadcasted_iota(jnp.int32, (ROWS, COLUMNS), 1)
+    packed_columns = jnp.zeros((ROWS, COLUMNS), jnp.float32)
+    for c in range(COMPONENTS):
+        plane = rho[c]
+        halo_out[0, 2 * c : 2 * c + 2, :] = plane[0:2]
+        halo_out[1, 2 * c : 2 * c + 2, :] = plane[ROWS - 2 : ROWS]
+        first = pltpu.roll(plane, 2 * c, 1) if c else plane
+        last = pltpu.roll(plane, 66 + 2 * c, 1)
+        packed_columns = jnp.where((lane // 2) == c, first, packed_columns)
+        packed_columns = jnp.where((lane // 2) == 32 + c, last, packed_columns)
+        extended[c, 8 : 8 + ROWS, :] = plane
+    columns_out[...] = packed_columns
+
+    pl.semaphore_wait(barrier, KX_DEVICES * KY_DEVICES - 1)
+
+    def forward_target(step):
+        c = (component + 1 + step) % COMPONENTS
+        return c, 2 * (c // 8) + upper, c % 8
+
+    def send_forward(step, carry):
+        c, target_i, target_j = forward_target(step)
+        slot = i * 4 + j % 4
+        target = lines.at[j % 4, pl.ds(pl.multiple_of(ROWS * i, ROWS), ROWS), :]
+        own = (target_i == i) & (target_j == j)
+
+        @pl.when(jnp.logical_not(own))
+        def _():
+            remote(rho.at[c], target, send_sem.at[step], line_sem.at[slot], (target_i, target_j)).start()
+
+        @pl.when(own)
+        def _():
+            pltpu.make_async_copy(rho.at[c], target, line_sem.at[slot]).start()
+
+        return carry
+
+    lax.fori_loop(0, COMPONENTS, send_forward, 0)
+
+    before_i, after_i = (i + KX_DEVICES - 1) % KX_DEVICES, (i + 1) % KX_DEVICES
+    before_j, after_j = (j + KY_DEVICES - 1) % KY_DEVICES, (j + 1) % KY_DEVICES
+    halo_copies = [
+        remote(halo_out.at[0], halo_in.at[1], halo_send.at[0], halo_recv.at[0], (before_i, j)),
+        remote(halo_out.at[1], halo_in.at[0], halo_send.at[1], halo_recv.at[1], (after_i, j)),
+        remote(columns_out, columns_in.at[1], halo_send.at[2], halo_recv.at[2], (i, before_j)),
+        remote(columns_out, columns_in.at[0], halo_send.at[3], halo_recv.at[3], (i, after_j)),
+    ]
+    for copy in halo_copies:
+        copy.start()
+
+    tables[0].wait()
+    high = interaction[...].astype(jnp.bfloat16)
+    rest = interaction[...] - high.astype(jnp.float32)
+    middle = rest.astype(jnp.bfloat16)
+    low = (rest - middle.astype(jnp.float32)).astype(jnp.bfloat16)
+    picked = matmul(jnp.concatenate([high, middle, low], axis=0), pick_table_vmem[...])
+    weights_own[...] = picked[0:16] + picked[16:32] + picked[32:48]
+
+    block = jnp.where(upper == 0, j, 7 - j)
+    sends_weights = half == block // 2
+    sends_special = ((j == 4) & (half == 0)) | ((j == 0) & (half == 1))
+    special_group = 1 - upper
+
+    def send_weights(step, carry):
+        target_j = 4 * upper + step
+        target = weights.at[pl.ds(pl.multiple_of(16 * (block % 2), 16), 16), :]
+
+        @pl.when(sends_weights & (target_j != j))
+        def _():
+            remote(
+                weights_own, target, weight_send.at[step], weight_recv.at[block % 2], (i, target_j)
+            ).start()
+
+        @pl.when(sends_weights & (target_j == j))
+        def _():
+            pltpu.make_async_copy(weights_own, target, weight_recv.at[block % 2]).start()
+
+        @pl.when(sends_special)
+        def _():
+            remote(
+                weights_own.at[pl.ds(0, 8), :], weight_special, weight_send.at[step], weight_recv.at[2],
+                (i, 4 * special_group + step),
+            ).start()
+
+        return carry
+
+    lax.fori_loop(0, 4, send_weights, 0)
+
+    for copy in halo_copies:
+        copy.wait_recv()
+    field_x = field[0]
+    field_y = field[1]
+    left_columns = columns_in[0]
+    right_columns = columns_in[1]
+    carriers_part = jnp.zeros((ROWS, COLUMNS), jnp.float32)
+    current_x_part = jnp.zeros((ROWS, COLUMNS), jnp.float32)
+    current_y_part = jnp.zeros((ROWS, COLUMNS), jnp.float32)
+    for c in range(COMPONENTS):
+        extended[c, 6:8, :] = halo_in[0, 2 * c : 2 * c + 2, :]
+        extended[c, 8 + ROWS : 10 + ROWS, :] = halo_in[1, 2 * c : 2 * c + 2, :]
+        plane = rho[c]
+        gradient_x = (
+            8.0 * (extended[c, 9 : 9 + ROWS, :] - extended[c, 7 : 7 + ROWS, :])
+            - (extended[c, 10 : 10 + ROWS, :] - extended[c, 6 : 6 + ROWS, :])
+        ) * (1.0 / 12.0)
+        ahead_edge = pltpu.roll(right_columns, (127 - 2 * c) % 128, 1)
+        ahead_two_edge = pltpu.roll(right_columns, (126 - 2 * c) % 128, 1)
+        behind_edge = pltpu.roll(left_columns, (63 - 2 * c) % 128, 1)
+        behind_two_edge = pltpu.roll(left_columns, 64 - 2 * c, 1)
+        ahead = jnp.where(lane >= 127, ahead_edge, pltpu.roll(plane, 127, 1))
+        ahead_two = jnp.where(lane >= 126, ahead_two_edge, pltpu.roll(plane, 126, 1))
+        behind = jnp.where(lane < 1, behind_edge, pltpu.roll(plane, 1, 1))
+        behind_two = jnp.where(lane < 2, behind_two_edge, pltpu.roll(plane, 2, 1))
+        gradient_y = (8.0 * (ahead - behind) - (ahead_two - behind_two)) * (1.0 / 12.0)
+        drift = field_x * gradient_x + field_y * gradient_y
+        if c < 4:
+            current_x_part = current_x_part - energies[c] * gradient_x
+            current_y_part = current_y_part - energies[c] * gradient_y
+            static_part[c] = energies[c]
+        else:
+            drift = drift - DEPHASING * plane
+            static_part[c] = field_x * dipole_x[c - 4] + field_y * dipole_y[c - 4]
+        if c in (2, 3):
+            carriers_part = carriers_part + plane
+        out[c] = drift
+
+    def lane_sums(part):
+        folded = part[0:8] + part[8:16] + part[16:24] + part[24:32]
+        return jnp.sum(folded, axis=0, keepdims=True)
+
+    sums_kx[i] = jnp.concatenate(
+        [
+            lane_sums(carriers_part), lane_sums(current_x_part), lane_sums(current_y_part),
+            jnp.zeros((5, COLUMNS), jnp.float32),
+        ],
+        axis=0,
+    )
+
+    def send_sums_kx(step, carry):
+        target = (i + 1 + step) % KX_DEVICES
+        remote(sums_kx.at[i], sums_kx.at[i], sum_send.at[step], sum_recv.at[i], (target, j)).start()
+        return carry
+
+    lax.fori_loop(0, KX_DEVICES - 1, send_sums_kx, 0)
+
+    def await_line(slot, carry):
+        await_bytes(
+            lines.at[slot % 4, pl.ds(pl.multiple_of(ROWS * (slot // 4), ROWS), ROWS), :], line_sem.at[slot]
+        )
+        return carry
+
+    lax.fori_loop(0, COMPONENTS, await_line, 0)
+    whole_lines = jnp.concatenate([lines[0], lines[1], lines[2], lines[3]], axis=1)
+    turned[...] = table_by_columns(kx_forward[upper], whole_lines)
+
+    own_rows = pl.ds(pl.multiple_of(64 * half, 64), 64)
+    other_rows = pl.ds(pl.multiple_of(64 * (1 - half), 64), 64)
+    partner = (2 * chip_y + 1 - half, j)
+    outward = remote(turned.at[other_rows, :], turned_in, pair_send.at[0], pair_recv.at[0], partner)
+    outward.start()
+
+    def await_sums_kx(step, carry):
+        source = (i + 1 + step) % KX_DEVICES
+        await_bytes(sums_kx.at[source], sum_recv.at[source])
+        return carry
+
+    lax.fori_loop(0, KX_DEVICES - 1, await_sums_kx, 0)
+    sums_ky[j] = (sums_kx[0] + sums_kx[1]) + (sums_kx[2] + sums_kx[3])
+
+    def send_sums_ky(step, carry):
+        target = (j + 1 + step) % KY_DEVICES
+        remote(
+            sums_ky.at[j], sums_ky.at[j], sum_send.at[3 + step], sum_recv.at[KX_DEVICES + j], (i, target)
+        ).start()
+        return carry
+
+    lax.fori_loop(0, KY_DEVICES - 1, send_sums_ky, 0)
+
+    await_bytes(weights.at[pl.ds(0, 16), :], weight_recv.at[0])
+    await_bytes(weights.at[pl.ds(16, 16), :], weight_recv.at[1])
+
+    @pl.when(half == upper)
+    def _():
+        await_bytes(weight_special, weight_recv.at[2])
+
+    @pl.when(half != upper)
+    def _():
+        weight_special[...] = jnp.zeros_like(weight_special)
+
+    tables[1].wait()
+    tables[2].wait()
+    weight_rows = weights[...]
+    special = jnp.concatenate([weight_special[0:1, :]] * 32, axis=0)
+    row_at = lax.broadcasted_iota(jnp.int32, (32, 640), 0)
+    at_special = (row_at == 16 * upper) & (half == upper)
+    weight_rows = jnp.concatenate([weight_rows, jnp.where(at_special, special, weight_rows)], axis=0)
+    lane_at = lax.broadcasted_iota(jnp.int32, (64, 128), 1)
+    weight_sine = jnp.where(lane_at == 0, weight_rows[:, 512:640], weight_rows[:, 0:128])
+    weight_first = jnp.concatenate([weight_rows[:, 0:128], weight_sine], axis=1)
+    weight_second = jnp.concatenate([weight_rows[:, 128:256]] * 2, axis=1)
+    weight_third = jnp.concatenate([weight_rows[:, 256:512]] * 2, axis=1)
+
+    outward.wait_recv()
+    sign = jnp.where(half == 0, 1.0, -1.0)
+    own = turned[own_rows, :]
+    other = turned_in[...]
+    even = own + other
+    odd = sign * (own - other)
+    first = rows_by_table(even[:, :256] + even[:, 256:], short_table[0, 0, :256], short_table[0, 1, :256])
+    second = rows_by_table(even[:, :256] - even[:, 256:], short_table[0, 0, 256:], short_table[0, 1, 256:])
+    third = rows_by_table(odd, long_table[0, 0], long_table[0, 1])
+    first = rows_by_table(first * weight_first, short_table[1, 0, :256], short_table[1, 1, :256])
+    second = rows_by_table(second * weight_second, short_table[1, 0, 256:], short_table[1, 1, 256:])
+    odd = sign * rows_by_table(third * weight_third, long_table[1, 0], long_table[1, 1])
+    even = jnp.concatenate([first + second, first - second], axis=1)
+    outward.wait_send()
+    turned[own_rows, :] = even - odd
+    back[own_rows, :] = even + odd
+    homeward = remote(turned.at[own_rows, :], back.at[own_rows, :], pair_send.at[1], pair_recv.at[1], partner)
+    homeward.start()
+
+    def await_sums_ky(step, carry):
+        source = (j + 1 + step) % KY_DEVICES
+        await_bytes(sums_ky.at[source], sum_recv.at[KX_DEVICES + source])
+        return carry
+
+    lax.fori_loop(0, KY_DEVICES - 1, await_sums_ky, 0)
+    totals = sums_ky[0]
+    for source in range(1, KY_DEVICES):
+        totals = totals + sums_ky[source]
+    point_total = ROWS * COLUMNS * KX_DEVICES * KY_DEVICES
+    means = jnp.sum(totals, axis=1, keepdims=True) * (1.0 / point_total)
+    screen = 1.0 / (1.0 + SHIELDING_LEVEL * means[0:1, :])
+    field_out[0] = field_x - COUPLING * jnp.sum(means[1:2, :])
+    field_out[1] = field_y - COUPLING * jnp.sum(means[2:3, :])
+
+    await_bytes(back.at[other_rows, :], pair_recv.at[1])
+    convolved = table_by_columns(kx_back[upper], back[...])
+    for quarter in range(4):
+        final[quarter] = convolved[:, 128 * quarter : 128 * quarter + 128]
+
+    def send_back(step, carry):
+        slot = (4 * i + j % 4 + 1 + step) % 16
+        target_i = slot // 4
+        target_j = 4 * half + slot % 4
+        source = final.at[slot % 4, pl.ds(pl.multiple_of(ROWS * target_i, ROWS), ROWS), :]
+        own_target = (target_i == i) & (target_j == j)
+
+        @pl.when(jnp.logical_not(own_target))
+        def _():
+            remote(
+                source, conv.at[component], return_send.at[step], return_recv.at[component],
+                (target_i, target_j),
+            ).start()
+
+        @pl.when(own_target)
+        def _():
+            pltpu.make_async_copy(source, conv.at[component], return_recv.at[component]).start()
+
+        return carry
+
+    lax.fori_loop(0, COMPONENTS, send_back, 0)
+
+    def await_back(c, carry):
+        await_bytes(conv.at[c], return_recv.at[c])
+        return carry
+
+    lax.fori_loop(0, COMPONENTS, await_back, 0)
+
+    def rotate(group, carry):
+        rows = pl.ds(pl.multiple_of(8 * group, 8), 8)
+        coupled = [static_part[c, rows, :] - screen * conv[c, rows, :] for c in range(COMPONENTS)]
+        state = [rho[c, rows, :] for c in range(COMPONENTS)]
+        rotation = commutator_planes(coupled, state)
+        for c in range(COMPONENTS):
+            out[c, rows, :] = out[c, rows, :] + rotation[c]
+        return carry
+
+    lax.fori_loop(0, ROWS // 8, rotate, 0)
+
+    def drain(step, carry):
+        c, target_i, target_j = forward_target(step)
+
+        @pl.when(jnp.logical_not((target_i == i) & (target_j == j)))
+        def _():
+            await_bytes(rho.at[c], send_sem.at[step])
+
+        slot = (4 * i + j % 4 + 1 + step) % 16
+
+        @pl.when(jnp.logical_not((slot // 4 == i) & (4 * half + slot % 4 == j)))
+        def _():
+            await_bytes(conv.at[component], return_send.at[step])
+
+        return carry
+
+    lax.fori_loop(0, COMPONENTS, drain, 0)
+
+    def drain_weights(step, carry):
+        @pl.when(sends_weights & (4 * upper + step != j))
+        def _():
+            await_bytes(weights_own, weight_send.at[step])
+
+        @pl.when(sends_special)
+        def _():
+            await_bytes(weight_special, weight_send.at[step])
+
+        return carry
+
+    lax.fori_loop(0, 4, drain_weights, 0)
+
+    def drain_sums(step, carry):
+        await_bytes(sums_kx.at[0], sum_send.at[step])
+        return carry
+
+    lax.fori_loop(0, KX_DEVICES + KY_DEVICES - 2, drain_sums, 0)
+    for copy in halo_copies:
+        copy.wait_send()
+    homeward.wait_send()
+
+
+def commutator_planes(coupled, state):
+    coupled_real, coupled_imaginary = unpack(coupled)
+    state_real, state_imaginary = unpack(state)
+
+    def real_part(row, column):
+        return product_sum(
+            [
+                term
+                for middle in range(4)
+                for term in (
+                    (1.0, coupled_real[row][middle], state_real[middle][column]),
+                    (-1.0, coupled_imaginary[row][middle], state_imaginary[middle][column]),
+                    (-1.0, state_real[row][middle], coupled_real[middle][column]),
+                    (1.0, state_imaginary[row][middle], coupled_imaginary[middle][column]),
+                )
+            ]
+        )
+
+    def imaginary_part(row, column):
+        if row == column:
+            return 2.0 * product_sum(
+                [
+                    term
+                    for middle in range(4)
+                    if middle != row
+                    for term in (
+                        (1.0, coupled_real[row][middle], state_imaginary[middle][column]),
+                        (1.0, coupled_imaginary[row][middle], state_real[middle][column]),
+                    )
+                ]
+            )
+        return product_sum(
+            [
+                term
+                for middle in range(4)
+                for term in (
+                    (1.0, coupled_real[row][middle], state_imaginary[middle][column]),
+                    (1.0, coupled_imaginary[row][middle], state_real[middle][column]),
+                    (-1.0, state_real[row][middle], coupled_imaginary[middle][column]),
+                    (-1.0, state_imaginary[row][middle], coupled_real[middle][column]),
+                )
+            ]
+        )
+
+    return (
+        [imaginary_part(band, band) for band in range(4)]
+        + [imaginary_part(row, column) for row, column in BAND_PAIRS]
+        + [-real_part(row, column) for row, column in BAND_PAIRS]
+    )
+
+
+def constant_tables():
+    forward, backward = [], []
+    for upper in range(2):
+        table = kx_table(upper)
+        for tables, values in ((forward, table), (backward, table.T)):
+            high, low = split_table(values)
+            tables.append(np.concatenate([high, high, low], axis=1))
+    first, second, third = ky_tables()
+    short = [np.concatenate([first, second]), np.concatenate([first.T, second.T])]
+    long = [third, third.T]
+    return (
+        np.stack(forward),
+        np.stack(backward),
+        np.stack([np.stack(split_table(values)) for values in short]),
+        np.stack([np.stack(split_table(values)) for values in long]),
+        pick_table().astype(ml_dtypes.bfloat16),
+    )
+
+
+def section_body(packed_state_matrix, energies, dipole_x, dipole_y, interaction, driving_field):
+    tables = [jnp.asarray(table) for table in constant_tables()]
+    vmem = pl.BlockSpec(memory_space=pltpu.VMEM)
+    smem = pl.BlockSpec(memory_space=pltpu.SMEM)
+    anywhere = pl.BlockSpec(memory_space=pl.ANY)
+    f32 = jnp.float32
+    dma = pltpu.SemaphoreType.DMA
+    plane_stack = (COMPONENTS, ROWS, COLUMNS)
+    return pl.pallas_call(
+        section_kernel,
+        out_shape=(
+            jax.ShapeDtypeStruct(plane_stack, f32),
+            jax.ShapeDtypeStruct((2,), f32),
+        ),
+        in_specs=[vmem] * 5 + [smem] + [vmem] * 2 + [anywhere] * 3,
+        out_specs=(vmem, smem),
+        scratch_shapes=[
+            pltpu.VMEM((4, 128, 128), f32),
+            pltpu.VMEM(plane_stack, f32),
+            pltpu.VMEM((2, 32, COLUMNS), f32),
+            pltpu.VMEM((2, 32, COLUMNS), f32),
+            pltpu.VMEM((ROWS, COLUMNS), f32),
+            pltpu.VMEM((2, ROWS, COLUMNS), f32),
+            pltpu.VMEM((COMPONENTS, 48, COLUMNS), f32),
+            pltpu.VMEM((16, 640), f32),
+            pltpu.VMEM((32, 640), f32),
+            pltpu.VMEM((8, 640), f32),
+            pltpu.VMEM((128, 512), f32),
+            pltpu.VMEM((64, 512), f32),
+            pltpu.VMEM((128, 512), f32),
+            pltpu.VMEM((4, 128, 128), f32),
+            pltpu.VMEM((KX_DEVICES, 8, COLUMNS), f32),
+            pltpu.VMEM((KY_DEVICES, 8, COLUMNS), f32),
+            pltpu.VMEM(plane_stack, f32),
+            pltpu.VMEM((2, 2, 512, 256), jnp.bfloat16),
+            pltpu.VMEM((2, 2, 512, 512), jnp.bfloat16),
+            pltpu.VMEM((1024, 640), jnp.bfloat16),
+            dma((3,)),
+            dma((16,)),
+            dma((16,)),
+            dma((4,)),
+            dma((4,)),
+            dma((4,)),
+            dma((3,)),
+            dma((2,)),
+            dma((2,)),
+            dma((16,)),
+            dma((16,)),
+            dma((10,)),
+            dma((12,)),
+        ],
+        compiler_params=pltpu.CompilerParams(
+            collective_id=0, has_side_effects=True, vmem_limit_bytes=40 * 1024 * 1024
+        ),
+        cost_estimate=pl.CostEstimate(flops=1_200_000_000, bytes_accessed=6_000_000, transcendentals=0),
+    )(packed_state_matrix, energies, dipole_x, dipole_y, interaction, driving_field, *tables)
+
+
 def solution(mesh):
     in_specs = (
         P(None, "kx", "ky"),
@@ -249,4 +838,5 @@
         P(),
     )
     out_specs = (P(None, "kx", "ky"), P())
-    return jax.shard_map(body, mesh=mesh, in_specs=in_specs, out_specs=out_specs, check_vma=False)
+    chosen = section_body if fits_section_kernel(mesh) else body
+    return jax.shard_map(chosen, mesh=mesh, in_specs=in_specs, out_specs=out_specs, check_vma=False)

time: 192 us -> 47.6 us (0.25)
  waiting for transfers between devices: 55.3 us -> 0 us
  blocking collectives: 41.2 us -> 0 us
  Pallas kernels: 0 us -> 34.1 us
  matrix products: 24.1 us -> 0 us
  starting transfers between devices: 22.9 us -> 0 us
  local copies, waits for them, and re-layouts: 34 us -> 12.3 us
  other arithmetic: 12.6 us -> 0 us
    psum x1 -> x0, blocking collectives: 41.2 us -> none  [collect_moments(): return lax.psum(local_sums, ('kx', 'ky')) / primitive_tile_total]
    all_to_all x4 -> x0, waiting for transfers between devices: 39.1 us -> none  [the longest x1 14.1 us: convolve(): lax.all_to_all(joined, 'ky', split_axis=2, concat_axis=3, tiled=True)]
    pallas_call x0 -> x1, Pallas kernels: none -> 34.1 us  [section_body(): pl.pallas_call(section_kernel, out_shape=(jax.ShapeDtypeStruct(plane_stac...]
    dot_general x28 -> x0, matrix products: 24.1 us -> none  [the longest x7 6.84 us: complex_contract(): contract(einsum_form, data_imaginary, table_imaginary)]
    ppermute x4 -> x0, waiting for transfers between devices: 16.2 us -> none  [the longest x2 14.4 us: with_halo(): after = lax.ppermute(initial, axis, down)]
    all_to_all x4 -> x0, starting transfers between devices: 15.9 us -> none  [the longest x1 5.16 us: convolve(): lax.all_to_all(joined, 'ky', split_axis=2, concat_axis=3, tiled=True)]
    another operation x6 -> x0, local copies, waits for them, and re-layouts: 8.32 us -> none  [the longest x3 6.88 us: convolve(): jnp.stack([line_real, line_imaginary])]
    ppermute x4 -> x0, starting transfers between devices: 7.05 us -> none  [the longest x2 7.04 us: with_halo(): after = lax.ppermute(initial, axis, down)]
  transfers between devices with their start and end apart: 8 -> 0, of which waited for: 7 -> 0; matrix products, arithmetic and copies ran while one was open for 2% -> 0% of each run, Pallas kernels for 0% -> 0%
where the time goes in v1:
time: 47.6 us; the launch traced here: 47.1 us
  Pallas kernels  34.1 us (72%)
  local copies, waits for them, and re-layouts  12.3 us (26%)
  between operations  0.66 us (1%)
    pallas_call x1, Pallas kernels, section_body(): pl.pallas_call(section_kernel, out_shape=(jax.ShapeDtypeStruct(plane_stac...  34.1 us
    unnamed x24, local copies, waits for them, and re-layouts  12.3 us

profile of v1, /device:TPU:0, one launch (start us, length us, event | category | flops | bytes accessed | tf_op | source)
XLA Modules:
  0.0 47.1 jit_solution(4697344035997365039)
XLA Ops:
  0.6 0.0 copy-start
  0.6 1.6 %copy-done = bf16[2,2,512,512]{3,2,1,0:T(8,128)(2,1)S(1)} copy-done((bf16[2,2,512,512]{3,2,1,0:T(8,128)(2,1)S(1)}, bf16[2,2,512,512]{3,2,1,0:T(8,128)(2,1)}, u32[]{:S(2)}) %copy-start) | copy-done | bytes 2097176
  2.2 0.0 copy-start.1
  2.2 1.3 %copy-done.1 = bf16[1024,640]{1,0:T(8,128)(2,1)S(1)} copy-done((bf16[1024,640]{1,0:T(8,128)(2,1)S(1)}, bf16[1024,640]{1,0:T(8,128)(2,1)}, u32[]{:S(2)}) %copy-start.1) | copy-done | bytes 1310744
  3.5 0.0 copy-start.2
  3.5 1.2 %copy-done.2 = bf16[2,2,512,256]{3,2,1,0:T(8,128)(2,1)S(1)} copy-done((bf16[2,2,512,256]{3,2,1,0:T(8,128)(2,1)S(1)}, bf16[2,2,512,256]{3,2,1,0:T(8,128)(2,1)}, u32[]{:S(2)}) %copy-start.2) | copy-done | bytes 1048600
  4.8 0.0 copy-start.3
  4.8 0.9 %copy-done.3 = f32[16,32,128]{2,1,0:T(8,128)S(1)} copy-done((f32[16,32,128]{2,1,0:T(8,128)S(1)}, f32[16,32,128]{2,1,0:T(8,128)}, u32[]{:S(2)}) %copy-start.3) | copy-done | bytes 262168
  5.7 0.0 copy-start.4
  5.7 0.9 %copy-done.4 = f32[12,32,128]{2,1,0:T(8,128)S(1)} copy-done((f32[12,32,128]{2,1,0:T(8,128)S(1)}, f32[12,32,128]{2,1,0:T(8,128)}, u32[]{:S(2)}) %copy-start.4) | copy-done | bytes 196632
  6.6 0.0 copy-start.5
  6.6 0.9 %copy-done.5 = f32[12,32,128]{2,1,0:T(8,128)S(1)} copy-done((f32[12,32,128]{2,1,0:T(8,128)S(1)}, f32[12,32,128]{2,1,0:T(8,128)}, u32[]{:S(2)}) %copy-start.5) | copy-done | bytes 196632
  7.6 0.0 copy-start.6
  7.6 0.9 %copy-done.6 = bf16[2,128,384]{2,1,0:T(8,128)(2,1)S(1)} copy-done((bf16[2,128,384]{2,1,0:T(8,128)(2,1)S(1)}, bf16[2,128,384]{2,1,0:T(8,128)(2,1)}, u32[]{:S(2)}) %copy-start.6) | copy-done | bytes 196632
  8.5 0.0 copy-start.7
  8.5 0.9 %copy-done.7 = bf16[2,128,384]{2,1,0:T(8,128)(2,1)S(1)} copy-done((bf16[2,128,384]{2,1,0:T(8,128)(2,1)S(1)}, bf16[2,128,384]{2,1,0:T(8,128)(2,1)}, u32[]{:S(2)}) %copy-start.7) | copy-done | bytes 196632
  9.4 0.0 copy-start.8
  9.4 0.8 %copy-done.8 = f32[4,32,128]{2,1,0:T(8,128)S(1)} copy-done((f32[4,32,128]{2,1,0:T(8,128)S(1)}, f32[4,32,128]{2,1,0:T(8,128)}, u32[]{:S(2)}) %copy-start.8) | copy-done | bytes 65560
  10.3 0.0 copy-start.9
  10.3 0.8 %copy-done.9 = f32[16,1024]{1,0:T(8,128)S(1)} copy-done((f32[16,1024]{1,0:T(8,128)S(1)}, f32[16,1024]{1,0:T(8,128)}, u32[]{:S(2)}) %copy-start.9) | copy-done | bytes 65560
  11.1 0.0 copy-start.10
  11.1 0.7 %copy-done.10 = f32[2]{0:T(128)S(1)} copy-done((f32[2]{0:T(128)S(1)}, f32[2]{0:T(128)}, u32[]{:S(2)}) %copy-start.10) | copy-done | bytes 32
  11.8 34.1 %shard_map.122 = (f32[16,32,128]{2,1,0:T(8,128)S(1)}, f32[2]{0:T(128)S(1)}) custom-call(f32[16,32,128]{2,1,0:T(8,128)S(1)} %copy-done.3, f32[4,32,128]{2,1,0:T(8,128)S(1)} %copy-done.8, f32[12,32,128]{2,1,0:T(8,128)S(1)} %copy-done.4, f32[12,32,128]{2,1,0:T(8,128)S(1)} %copy-done.5, f32[16,1024]{1,0:T(8,128)S(1)} %copy-done.9, f32[2]{0:T(128)S(1)} %copy-done.10, ...), custom_call_target="tpu_custom_call" | custom-call | flops 1200000000 | bytes 6000000 | tf_op jit(solution)/shard_map/pallas_call | solution.py:781
  45.9 0.7 %copy.15 = f32[16,32,128]{2,1,0:T(8,128)} copy(f32[16,32,128]{2,1,0:T(8,128)S(1)} %get-tuple-element.4) | data formatting | bytes 524288
  46.6 0.5 %copy.16 = f32[2]{0:T(128)} copy(f32[2]{0:T(128)S(1)} %get-tuple-element.5) | data formatting | bytes 16
Async XLA Ops:
  0.6 1.6 %copy-start = (bf16[2,2,512,512]{3,2,1,0:T(8,128)(2,1)S(1)}, bf16[2,2,512,512]{3,2,1,0:T(8,128)(2,1)}, u32[]{:S(2)}) copy-start(bf16[2,2,512,512]{3,2,1,0:T(8,128)(2,1)} %constant.13.clone.ky_long) | copy-start | bytes 6291460
  2.2 1.3 %copy-start.1 = (bf16[1024,640]{1,0:T(8,128)(2,1)S(1)}, bf16[1024,640]{1,0:T(8,128)(2,1)}, u32[]{:S(2)}) copy-start(bf16[1024,640]{1,0:T(8,128)(2,1)} %constant.14.clone.pick) | copy-start | bytes 3932164
  3.5 1.2 %copy-start.2 = (bf16[2,2,512,256]{3,2,1,0:T(8,128)(2,1)S(1)}, bf16[2,2,512,256]{3,2,1,0:T(8,128)(2,1)}, u32[]{:S(2)}) copy-start(bf16[2,2,512,256]{3,2,1,0:T(8,128)(2,1)} %constant.12.clone.ky_short) | copy-start | bytes 3145732
  4.8 0.9 %copy-start.3 = (f32[16,32,128]{2,1,0:T(8,128)S(1)}, f32[16,32,128]{2,1,0:T(8,128)}, u32[]{:S(2)}) copy-start(f32[16,32,128]{2,1,0:T(8,128)} %rho.1) | copy-start | bytes 786436
  5.7 0.9 %copy-start.4 = (f32[12,32,128]{2,1,0:T(8,128)S(1)}, f32[12,32,128]{2,1,0:T(8,128)}, u32[]{:S(2)}) copy-start(f32[12,32,128]{2,1,0:T(8,128)} %dipole_x.1) | copy-start | bytes 589828
  6.6 0.9 %copy-start.5 = (f32[12,32,128]{2,1,0:T(8,128)S(1)}, f32[12,32,128]{2,1,0:T(8,128)}, u32[]{:S(2)}) copy-start(f32[12,32,128]{2,1,0:T(8,128)} %dipole_y.1) | copy-start | bytes 589828
  7.6 0.9 %copy-start.6 = (bf16[2,128,384]{2,1,0:T(8,128)(2,1)S(1)}, bf16[2,128,384]{2,1,0:T(8,128)(2,1)}, u32[]{:S(2)}) copy-start(bf16[2,128,384]{2,1,0:T(8,128)(2,1)} %constant.11.clone.kx_back) | copy-start | bytes 589828
  8.5 0.9 %copy-start.7 = (bf16[2,128,384]{2,1,0:T(8,128)(2,1)S(1)}, bf16[2,128,384]{2,1,0:T(8,128)(2,1)}, u32[]{:S(2)}) copy-start(bf16[2,128,384]{2,1,0:T(8,128)(2,1)} %constant.10.clone.kx_forward) | copy-start | bytes 589828
  9.4 0.8 %copy-start.8 = (f32[4,32,128]{2,1,0:T(8,128)S(1)}, f32[4,32,128]{2,1,0:T(8,128)}, u32[]{:S(2)}) copy-start(f32[4,32,128]{2,1,0:T(8,128)} %energies.1) | copy-start | bytes 196612
  10.3 0.8 %copy-start.9 = (f32[16,1024]{1,0:T(8,128)S(1)}, f32[16,1024]{1,0:T(8,128)}, u32[]{:S(2)}) copy-start(f32[16,1024]{1,0:T(8,128)} %interaction.1) | copy-start | bytes 196612
  11.1 0.7 %copy-start.10 = (f32[2]{0:T(128)S(1)}, f32[2]{0:T(128)}, u32[]{:S(2)}) copy-start(f32[2]{0:T(128)} %field.1) | copy-start | bytes 28

commit v2 on v1

--- a/solution.py
+++ b/solution.py
@@ -335,9 +335,10 @@
 
 
 def section_kernel(
-    rho, energies, dipole_x, dipole_y, interaction, field,
-    kx_forward, kx_back, ky_short, ky_long, pick,
+    rho_far, energies_far, dipole_x_far, dipole_y_far, interaction_far, field,
+    kx_forward_far, kx_back_far, ky_short, ky_long, pick,
     out, field_out,
+    rho, energies, dipole_x, dipole_y, interaction, kx_forward, kx_back,
     lines, conv, halo_out, halo_in, columns_out, columns_in, extended,
     weights_own, weights, weight_special, turned, turned_in, back, final,
     sums_kx, sums_ky, static_part,
@@ -352,13 +353,25 @@
     upper = j // 4
     component = chip_y * 8 + j
 
-    tables = [
-        pltpu.make_async_copy(pick, pick_table_vmem, table_sem.at[0]),
-        pltpu.make_async_copy(ky_short, short_table, table_sem.at[1]),
-        pltpu.make_async_copy(ky_long, long_table, table_sem.at[2]),
+    fetches = [
+        pltpu.make_async_copy(source, target, table_sem.at[number])
+        for number, (source, target) in enumerate(
+            (
+                (rho_far, rho),
+                (interaction_far, interaction),
+                (pick, pick_table_vmem),
+                (energies_far, energies),
+                (dipole_x_far, dipole_x),
+                (dipole_y_far, dipole_y),
+                (kx_forward_far, kx_forward),
+                (ky_short, short_table),
+                (ky_long, long_table),
+                (kx_back_far, kx_back),
+            )
+        )
     ]
-    for table in tables:
-        table.start()
+    for fetch in fetches:
+        fetch.start()
 
     barrier = pltpu.get_barrier_semaphore()
 
@@ -382,6 +395,7 @@
     def await_bytes(ref, semaphore):
         pltpu.make_async_copy(ref, ref, semaphore).wait()
 
+    fetches[0].wait()
     lane = lax.broadcasted_iota(jnp.int32, (ROWS, COLUMNS), 1)
     packed_columns = jnp.zeros((ROWS, COLUMNS), jnp.float32)
     for c in range(COMPONENTS):
@@ -430,7 +444,8 @@
     for copy in halo_copies:
         copy.start()
 
-    tables[0].wait()
+    fetches[1].wait()
+    fetches[2].wait()
     high = interaction[...].astype(jnp.bfloat16)
     rest = interaction[...] - high.astype(jnp.float32)
     middle = rest.astype(jnp.bfloat16)
@@ -468,6 +483,8 @@
 
     lax.fori_loop(0, 4, send_weights, 0)
 
+    for fetch in fetches[3:6]:
+        fetch.wait()
     for copy in halo_copies:
         copy.wait_recv()
     field_x = field[0]
@@ -532,6 +549,7 @@
         return carry
 
     lax.fori_loop(0, COMPONENTS, await_line, 0)
+    fetches[6].wait()
     whole_lines = jnp.concatenate([lines[0], lines[1], lines[2], lines[3]], axis=1)
     turned[...] = table_by_columns(kx_forward[upper], whole_lines)
 
@@ -569,8 +587,8 @@
     def _():
         weight_special[...] = jnp.zeros_like(weight_special)
 
-    tables[1].wait()
-    tables[2].wait()
+    fetches[7].wait()
+    fetches[8].wait()
     weight_rows = weights[...]
     special = jnp.concatenate([weight_special[0:1, :]] * 32, axis=0)
     row_at = lax.broadcasted_iota(jnp.int32, (32, 640), 0)
@@ -617,6 +635,7 @@
     field_out[1] = field_y - COUPLING * jnp.sum(means[2:3, :])
 
     await_bytes(back.at[other_rows, :], pair_recv.at[1])
+    fetches[9].wait()
     convolved = table_by_columns(kx_back[upper], back[...])
     for quarter in range(4):
         final[quarter] = convolved[:, 128 * quarter : 128 * quarter + 128]
@@ -784,9 +803,16 @@
             jax.ShapeDtypeStruct(plane_stack, f32),
             jax.ShapeDtypeStruct((2,), f32),
         ),
-        in_specs=[vmem] * 5 + [smem] + [vmem] * 2 + [anywhere] * 3,
+        in_specs=[anywhere] * 5 + [smem] + [anywhere] * 5,
         out_specs=(vmem, smem),
         scratch_shapes=[
+            pltpu.VMEM(plane_stack, f32),
+            pltpu.VMEM((4, ROWS, COLUMNS), f32),
+            pltpu.VMEM((12, ROWS, COLUMNS), f32),
+            pltpu.VMEM((12, ROWS, COLUMNS), f32),
+            pltpu.VMEM((16, 1024), f32),
+            pltpu.VMEM((2, 128, 384), jnp.bfloat16),
+            pltpu.VMEM((2, 128, 384), jnp.bfloat16),
             pltpu.VMEM((4, 128, 128), f32),
             pltpu.VMEM(plane_stack, f32),
             pltpu.VMEM((2, 32, COLUMNS), f32),
@@ -807,7 +833,7 @@
             pltpu.VMEM((2, 2, 512, 256), jnp.bfloat16),
             pltpu.VMEM((2, 2, 512, 512), jnp.bfloat16),
             pltpu.VMEM((1024, 640), jnp.bfloat16),
-            dma((3,)),
+            dma((10,)),
             dma((16,)),
             dma((16,)),
             dma((4,)),
@@ -822,7 +848,7 @@
             dma((12,)),
         ],
         compiler_params=pltpu.CompilerParams(
-            collective_id=0, has_side_effects=True, vmem_limit_bytes=40 * 1024 * 1024
+            collective_id=0, has_side_effects=True, vmem_limit_bytes=64 * 1024 * 1024
         ),
         cost_estimate=pl.CostEstimate(flops=1_200_000_000, bytes_accessed=6_000_000, transcendentals=0),
     )(packed_state_matrix, energies, dipole_x, dipole_y, interaction, driving_field, *tables)

time: 47.6 us -> 37.8 us (0.79)
  local copies, waits for them, and re-layouts: 12.3 us -> 2.8 us
    unnamed x24 -> x2, local copies, waits for them, and re-layouts: 12.3 us -> 2.8 us
where the time goes in v2:
time: 37.8 us; the launch traced here: 37.6 us
  Pallas kernels  34.2 us (90%)
  local copies, waits for them, and re-layouts  2.8 us (7%)
  between operations  0.64 us (2%)
    pallas_call x1, Pallas kernels, section_body(): pl.pallas_call(section_kernel, out_shape=(jax.ShapeDtypeStruct(plane_stac...  34.2 us
    unnamed x2, local copies, waits for them, and re-layouts  2.8 us

profile of v2, /device:TPU:0, one launch (start us, length us, event | category | flops | bytes accessed | tf_op | source)
XLA Modules:
  0.0 37.6 jit_solution(6453244669810693895)
XLA Ops:
  0.6 34.2 %shard_map.122 = (f32[16,32,128]{2,1,0:T(8,128)}, f32[2]{0:T(128)}) custom-call(f32[16,32,128]{2,1,0:T(8,128)} %rho_far.1, f32[4,32,128]{2,1,0:T(8,128)} %energies_far.1, f32[12,32,128]{2,1,0:T(8,128)} %dipole_x_far.1, f32[12,32,128]{2,1,0:T(8,128)} %dipole_y_far.1, f32[16,1024]{1,0:T(8,128)} %interaction_far.1, f32[2]{0:T(128)} %field.1, ...), custom_call_target="tpu_custom_call" | custom-call | flops 1200000000 | bytes 6000000 | tf_op jit(solution)/shard_map/pallas_call | solution.py:800
  34.8 1.7 %copy.15 = f32[16,32,128]{2,1,0:T(8,128)} copy(f32[16,32,128]{2,1,0:T(8,128)} %get-tuple-element.4) | data formatting | bytes 524288
  36.5 1.1 %copy.16 = f32[2]{0:T(128)} copy(f32[2]{0:T(128)} %get-tuple-element.5) | data formatting | bytes 16

commit v3 on v2

--- a/solution.py
+++ b/solution.py
@@ -340,7 +340,7 @@
     out, field_out,
     rho, energies, dipole_x, dipole_y, interaction, kx_forward, kx_back,
     lines, conv, halo_out, halo_in, columns_out, columns_in, extended,
-    weights_own, weights, weight_special, turned, turned_in, back, final,
+    weights_own, weights, weight_special, turned, turned_in, back_out, back_in, final, leaving,
     sums_kx, sums_ky, static_part,
     short_table, long_table, pick_table_vmem,
     table_sem, send_sem, line_sem, halo_send, halo_recv, weight_send, weight_recv,
@@ -351,6 +351,8 @@
     chip_y = i // 2
     half = i % 2
     upper = j // 4
+    place_z = j // 2
+    parity = j % 2
     component = chip_y * 8 + j
 
     fetches = [
@@ -395,6 +397,38 @@
     def await_bytes(ref, semaphore):
         pltpu.make_async_copy(ref, ref, semaphore).wait()
 
+    pl.semaphore_wait(barrier, KX_DEVICES * KY_DEVICES - 1)
+
+    def toward(step):
+        across = (step + 1) % 2
+        number = jnp.where(across == 1, step // 2, 7 - step // 2)
+        target_z = 2 * ((place_z // 2 + across) % 2) + (place_z + number) % 2
+        target_x = (parity + number // 2) % 2
+        target_y = (chip_y + number // 4) % 2
+        return target_y, 2 * target_z + target_x
+
+    def forward_target(step):
+        target_y, target_j = toward(step)
+        return 8 * target_y + target_j, 2 * target_y + parity, target_j
+
+    def send_forward(step, carry):
+        c, target_i, target_j = forward_target(step)
+        slot = i * 4 + place_z
+        target = lines.at[place_z, pl.ds(pl.multiple_of(ROWS * i, ROWS), ROWS), :]
+        own = (target_i == i) & (target_j == j)
+
+        @pl.when(jnp.logical_not(own))
+        def _():
+            remote(rho_far.at[c], target, send_sem.at[step], line_sem.at[slot], (target_i, target_j)).start()
+
+        @pl.when(own)
+        def _():
+            pltpu.make_async_copy(rho_far.at[c], target, line_sem.at[slot]).start()
+
+        return carry
+
+    lax.fori_loop(0, COMPONENTS, send_forward, 0)
+
     fetches[0].wait()
     lane = lax.broadcasted_iota(jnp.int32, (ROWS, COLUMNS), 1)
     packed_columns = jnp.zeros((ROWS, COLUMNS), jnp.float32)
@@ -408,30 +442,6 @@
         packed_columns = jnp.where((lane // 2) == 32 + c, last, packed_columns)
         extended[c, 8 : 8 + ROWS, :] = plane
     columns_out[...] = packed_columns
-
-    pl.semaphore_wait(barrier, KX_DEVICES * KY_DEVICES - 1)
-
-    def forward_target(step):
-        c = (component + 1 + step) % COMPONENTS
-        return c, 2 * (c // 8) + upper, c % 8
-
-    def send_forward(step, carry):
-        c, target_i, target_j = forward_target(step)
-        slot = i * 4 + j % 4
-        target = lines.at[j % 4, pl.ds(pl.multiple_of(ROWS * i, ROWS), ROWS), :]
-        own = (target_i == i) & (target_j == j)
-
-        @pl.when(jnp.logical_not(own))
-        def _():
-            remote(rho.at[c], target, send_sem.at[step], line_sem.at[slot], (target_i, target_j)).start()
-
-        @pl.when(own)
-        def _():
-            pltpu.make_async_copy(rho.at[c], target, line_sem.at[slot]).start()
-
-        return carry
-
-    lax.fori_loop(0, COMPONENTS, send_forward, 0)
 
     before_i, after_i = (i + KX_DEVICES - 1) % KX_DEVICES, (i + 1) % KX_DEVICES
     before_j, after_j = (j + KY_DEVICES - 1) % KY_DEVICES, (j + 1) % KY_DEVICES
@@ -542,22 +552,31 @@
 
     lax.fori_loop(0, KX_DEVICES - 1, send_sums_kx, 0)
 
-    def await_line(slot, carry):
-        await_bytes(
-            lines.at[slot % 4, pl.ds(pl.multiple_of(ROWS * (slot // 4), ROWS), ROWS), :], line_sem.at[slot]
-        )
-        return carry
-
-    lax.fori_loop(0, COMPONENTS, await_line, 0)
-    fetches[6].wait()
-    whole_lines = jnp.concatenate([lines[0], lines[1], lines[2], lines[3]], axis=1)
-    turned[...] = table_by_columns(kx_forward[upper], whole_lines)
-
     own_rows = pl.ds(pl.multiple_of(64 * half, 64), 64)
     other_rows = pl.ds(pl.multiple_of(64 * (1 - half), 64), 64)
     partner = (2 * chip_y + 1 - half, j)
-    outward = remote(turned.at[other_rows, :], turned_in, pair_send.at[0], pair_recv.at[0], partner)
-    outward.start()
+    fetches[6].wait()
+
+    def quarter_at(step):
+        return 2 * ((place_z // 2 + step // 2) % 2) + (place_z + step) % 2
+
+    def pair_copy(quarter):
+        return remote(
+            turned.at[quarter, other_rows, :], turned_in.at[quarter], pair_send.at[quarter],
+            pair_recv.at[quarter], partner,
+        )
+
+    def turn_quarter(step, carry):
+        quarter = quarter_at(step)
+        for source in range(KX_DEVICES):
+            await_bytes(
+                lines.at[quarter, pl.ds(ROWS * source, ROWS), :], line_sem.at[4 * source + quarter]
+            )
+        turned[quarter] = table_by_columns(kx_forward[upper], lines[quarter])
+        pair_copy(quarter).start()
+        return carry
+
+    lax.fori_loop(0, 4, turn_quarter, 0)
 
     def await_sums_kx(step, carry):
         source = (i + 1 + step) % KX_DEVICES
@@ -600,24 +619,49 @@
     weight_second = jnp.concatenate([weight_rows[:, 128:256]] * 2, axis=1)
     weight_third = jnp.concatenate([weight_rows[:, 256:512]] * 2, axis=1)
 
-    outward.wait_recv()
-    sign = jnp.where(half == 0, 1.0, -1.0)
-    own = turned[own_rows, :]
-    other = turned_in[...]
-    even = own + other
-    odd = sign * (own - other)
-    first = rows_by_table(even[:, :256] + even[:, 256:], short_table[0, 0, :256], short_table[0, 1, :256])
-    second = rows_by_table(even[:, :256] - even[:, 256:], short_table[0, 0, 256:], short_table[0, 1, 256:])
-    third = rows_by_table(odd, long_table[0, 0], long_table[0, 1])
+    for quarter in range(4):
+        await_bytes(turned_in.at[quarter], pair_recv.at[quarter])
+    is_first = half == 0
+    blocks = []
+    for quarter in range(4):
+        own = turned[quarter, own_rows, :]
+        other = turned_in[quarter]
+        blocks.append(jnp.where(is_first, own, other))
+        blocks.append(jnp.where(is_first, other, own))
+    even = [blocks[at] + blocks[at + 4] for at in range(4)]
+    odd = [blocks[at] - blocks[at + 4] for at in range(4)]
+
+    def beside(parts):
+        return jnp.concatenate(parts, axis=1)
+
+    first = rows_by_table(
+        beside([even[0] + even[2], even[1] + even[3]]), short_table[0, 0, :256], short_table[0, 1, :256]
+    )
+    second = rows_by_table(
+        beside([even[0] - even[2], even[1] - even[3]]), short_table[0, 0, 256:], short_table[0, 1, 256:]
+    )
+    third = rows_by_table(beside(odd), long_table[0, 0], long_table[0, 1])
     first = rows_by_table(first * weight_first, short_table[1, 0, :256], short_table[1, 1, :256])
     second = rows_by_table(second * weight_second, short_table[1, 0, 256:], short_table[1, 1, 256:])
-    odd = sign * rows_by_table(third * weight_third, long_table[1, 0], long_table[1, 1])
-    even = jnp.concatenate([first + second, first - second], axis=1)
-    outward.wait_send()
-    turned[own_rows, :] = even - odd
-    back[own_rows, :] = even + odd
-    homeward = remote(turned.at[own_rows, :], back.at[own_rows, :], pair_send.at[1], pair_recv.at[1], partner)
+    odd = rows_by_table(third * weight_third, long_table[1, 0], long_table[1, 1])
+    even = beside([first + second, first - second])
+    ahead_half, behind_half = even + odd, even - odd
+
+    def every_other(start):
+        return beside(
+            [
+                values[:, 128 * at : 128 * at + 128]
+                for values in (ahead_half, behind_half)
+                for at in (start, start + 2)
+            ]
+        )
+
+    at_even, at_odd = every_other(0), every_other(1)
+    back_out[...] = jnp.where(is_first, at_odd, at_even)
+    homeward = remote(back_out, back_in, pair_send.at[4], pair_recv.at[4], partner)
     homeward.start()
+    fetches[9].wait()
+    final[...] = table_by_columns(kx_back[upper, half], jnp.where(is_first, at_even, at_odd))
 
     def await_sums_ky(step, carry):
         source = (j + 1 + step) % KY_DEVICES
@@ -634,17 +678,19 @@
     field_out[0] = field_x - COUPLING * jnp.sum(means[1:2, :])
     field_out[1] = field_y - COUPLING * jnp.sum(means[2:3, :])
 
-    await_bytes(back.at[other_rows, :], pair_recv.at[1])
-    fetches[9].wait()
-    convolved = table_by_columns(kx_back[upper], back[...])
+    homeward.wait_recv()
+    convolved = final[...] + table_by_columns(kx_back[upper, 1 - half], back_in[...])
     for quarter in range(4):
-        final[quarter] = convolved[:, 128 * quarter : 128 * quarter + 128]
+        leaving[quarter] = convolved[:, 128 * quarter : 128 * quarter + 128]
+
+    def back_target(step):
+        quarter = quarter_at(2 * ((step + 1) % 2) + (step // 2) % 2)
+        target_i = 2 * ((chip_y + step // 8) % 2) + (half + step // 4) % 2
+        return target_i, quarter, 2 * quarter + half
 
     def send_back(step, carry):
-        slot = (4 * i + j % 4 + 1 + step) % 16
-        target_i = slot // 4
-        target_j = 4 * half + slot % 4
-        source = final.at[slot % 4, pl.ds(pl.multiple_of(ROWS * target_i, ROWS), ROWS), :]
+        target_i, quarter, target_j = back_target(step)
+        source = leaving.at[quarter, pl.ds(pl.multiple_of(ROWS * target_i, ROWS), ROWS), :]
         own_target = (target_i == i) & (target_j == j)
 
         @pl.when(jnp.logical_not(own_target))
@@ -686,9 +732,9 @@
         def _():
             await_bytes(rho.at[c], send_sem.at[step])
 
-        slot = (4 * i + j % 4 + 1 + step) % 16
-
-        @pl.when(jnp.logical_not((slot // 4 == i) & (4 * half + slot % 4 == j)))
+        back_i, _, back_j = back_target(step)
+
+        @pl.when(jnp.logical_not((back_i == i) & (back_j == j)))
         def _():
             await_bytes(conv.at[component], return_send.at[step])
 
@@ -717,6 +763,8 @@
     for copy in halo_copies:
         copy.wait_send()
     homeward.wait_send()
+    for quarter in range(4):
+        await_bytes(turned_in.at[quarter], pair_send.at[quarter])
 
 
 def commutator_planes(coupled, state):
@@ -774,9 +822,10 @@
     forward, backward = [], []
     for upper in range(2):
         table = kx_table(upper)
-        for tables, values in ((forward, table), (backward, table.T)):
-            high, low = split_table(values)
-            tables.append(np.concatenate([high, high, low], axis=1))
+        high, low = split_table(table)
+        forward.append(np.concatenate([high, high, low], axis=1))
+        halves = [split_table(table[rows].T) for rows in (slice(0, 64), slice(64, 128))]
+        backward.append(np.stack([np.concatenate([high, high, low], axis=1) for high, low in halves]))
     first, second, third = ky_tables()
     short = [np.concatenate([first, second]), np.concatenate([first.T, second.T])]
     long = [third, third.T]
@@ -812,7 +861,7 @@
             pltpu.VMEM((12, ROWS, COLUMNS), f32),
             pltpu.VMEM((16, 1024), f32),
             pltpu.VMEM((2, 128, 384), jnp.bfloat16),
-            pltpu.VMEM((2, 128, 384), jnp.bfloat16),
+            pltpu.VMEM((2, 2, 128, 192), jnp.bfloat16),
             pltpu.VMEM((4, 128, 128), f32),
             pltpu.VMEM(plane_stack, f32),
             pltpu.VMEM((2, 32, COLUMNS), f32),
@@ -823,7 +872,9 @@
             pltpu.VMEM((16, 640), f32),
             pltpu.VMEM((32, 640), f32),
             pltpu.VMEM((8, 640), f32),
-            pltpu.VMEM((128, 512), f32),
+            pltpu.VMEM((4, 128, 128), f32),
+            pltpu.VMEM((4, 64, 128), f32),
+            pltpu.VMEM((64, 512), f32),
             pltpu.VMEM((64, 512), f32),
             pltpu.VMEM((128, 512), f32),
             pltpu.VMEM((4, 128, 128), f32),
@@ -840,8 +891,8 @@
             dma((4,)),
             dma((4,)),
             dma((3,)),
-            dma((2,)),
-            dma((2,)),
+            dma((5,)),
+            dma((5,)),
             dma((16,)),
             dma((16,)),
             dma((10,)),

time: 37.8 us -> 37.2 us (0.984)
  Pallas kernels: 34.2 us -> 33.6 us
    pallas_call x1, Pallas kernels: 34.2 us -> 33.6 us  [section_body(): pl.pallas_call(section_kernel, out_shape=(jax.ShapeDtypeStruct(plane_stac...]
where the time goes in v3:
time: 37.2 us; the launch traced here: 37 us
  Pallas kernels  33.6 us (90%)
  local copies, waits for them, and re-layouts  2.8 us (8%)
  between operations  0.64 us (2%)
    pallas_call x1, Pallas kernels, section_body(): pl.pallas_call(section_kernel, out_shape=(jax.ShapeDtypeStruct(plane_stac...  33.6 us
    unnamed x2, local copies, waits for them, and re-layouts  2.8 us

profile of v3, /device:TPU:0, one launch (start us, length us, event | category | flops | bytes accessed | tf_op | source)
XLA Modules:
  0.0 37.0 jit_solution(4289465569908452693)
XLA Ops:
  0.6 33.6 %shard_map.122 = (f32[16,32,128]{2,1,0:T(8,128)}, f32[2]{0:T(128)}) custom-call(f32[16,32,128]{2,1,0:T(8,128)} %rho_far.1, f32[4,32,128]{2,1,0:T(8,128)} %energies_far.1, f32[12,32,128]{2,1,0:T(8,128)} %dipole_x_far.1, f32[12,32,128]{2,1,0:T(8,128)} %dipole_y_far.1, f32[16,1024]{1,0:T(8,128)} %interaction_far.1, f32[2]{0:T(128)} %field.1, ...), custom_call_target="tpu_custom_call" | custom-call | flops 1200000000 | bytes 6000000 | tf_op jit(solution)/shard_map/pallas_call | solution.py:849
  34.2 1.7 %copy.15 = f32[16,32,128]{2,1,0:T(8,128)} copy(f32[16,32,128]{2,1,0:T(8,128)} %get-tuple-element.4) | data formatting | bytes 524288
  35.9 1.1 %copy.16 = f32[2]{0:T(128)} copy(f32[2]{0:T(128)} %get-tuple-element.5) | data formatting | bytes 16
